TPU v7x, 32 devices: a whole 2x2x4 slice. The times are simulated.
32 devices in a mesh: groups: 2 (over x), dev: 8 (over z, y), sub: 2 (over core).
Axes of the slice: x: 2, y: 2, z: 4, core: 2. Of those that a mesh axis runs over, the one named last changes fastest.
Arguments:
- hidden_in: bfloat16 [2, 64, 6144], P(None, ('groups', 'dev', 'sub')), parts along dimension 1, may hold values from -6 to 6
- queries: bfloat16 [2, 64, 6144], P(None, ('groups', 'dev', 'sub')), parts along dimension 1, may hold values from -8 to 8
- key_new: bfloat16 [2, 64, 1024], P(None, ('groups', 'dev', 'sub')), parts along dimension 1, may hold values from -8 to 8
- value_new: bfloat16 [2, 64, 1024], P(None, ('groups', 'dev', 'sub')), parts along dimension 1, may hold values from -6 to 6
- key_cache: bfloat16 [2, 64, 64, 1024], P(None, ('groups', 'dev', 'sub')), parts along dimension 1, may hold values from -8 to 8
- value_cache: bfloat16 [2, 64, 64, 1024], P(None, ('groups', 'dev', 'sub')), parts along dimension 1, may hold values from -6 to 6
- cache_length: int32 [2, 64], P(None, ('groups', 'dev', 'sub')), parts along dimension 1, may hold values from 1 to 64, as said below
- expert_ids: int32 [2, 64, 2], P(None, ('groups', 'dev', 'sub')), parts along dimension 1, may hold values from 0 to 7, as said below
- route_logits: float32 [2, 64, 2], P(None, ('groups', 'dev', 'sub')), parts along dimension 1, may hold values from -6 to 6
- norm_gain: float32 [6144], replicated, may hold values from 0.1 to 1.9
- w_gate: bfloat16 [6144, 16384], P('sub', 'dev'), may hold values from -0.078125 to 0.078125
- w_up: bfloat16 [6144, 16384], P('sub', 'dev'), may hold values from -0.078125 to 0.078125
- w_down: bfloat16 [16384, 6144], P('dev', 'sub'), may hold values from -0.0625 to 0.0625
Outputs:
- layer_out: bfloat16 [2, 64, 6144], P(None, ('groups', 'dev', 'sub')), parts along dimension 1
There are 2 independent parts, one for each index of `groups`. A program takes and returns all parts, laid end to end along the dimension named above; an argument that names none is the same for every part. Nothing has to cross between parts.
Inputs may be any that keep to these rules, and one draw needn't show every extreme that they name: `cache_length`: in each micro-batch some row has exactly 64 filled slots. `expert_ids`: the two ids of a row differ. In each aligned block of 4 rows of a micro-batch (the rows of the devices sharing one index of dev), each expert below 2 is chosen by at most 3 rows and one of them by exactly 3; in some micro-batch one expert below 2 is chosen by 3 rows in every block.
All inputs are finite; a program needn't handle non-finite values.
Results may differ from a plain program's by a relative error of at most 0.005.
Values may be sent and summed in bfloat16 or wider, within the bound.
A program may use at most 128 MiB of HBM per device.

v0:
```python
import jax
import jax.numpy as jnp
from jax import lax
from jax.sharding import PartitionSpec as P

HEADS = 48
KV_HEADS = 8
HEAD_DIM = 128
EXP_FLIGHT = 2


masked_score = -1e30


def attend(queries, key_new, value_new, key_cache, value_cache, lengths):
    row_count = queries.shape[0]
    slot_count = key_cache.shape[1]
    groups = HEADS // KV_HEADS
    inv_root = 1.0 / HEAD_DIM**0.5
    query_heads = queries.reshape(row_count, KV_HEADS, groups, HEAD_DIM)
    cache_keys = key_cache.reshape(row_count, slot_count, KV_HEADS, HEAD_DIM)
    cache_values = value_cache.reshape(row_count, slot_count, KV_HEADS, HEAD_DIM)
    fresh_keys = key_new.reshape(row_count, KV_HEADS, HEAD_DIM)
    fresh_values = value_new.reshape(row_count, KV_HEADS, HEAD_DIM).astype(jnp.float32)
    cache_scores = (
        jnp.einsum("rkgd,rjkd->rkgj", query_heads, cache_keys, preferred_element_type=jnp.float32)
        * inv_root
    )
    fresh_scores = (
        jnp.einsum("rkgd,rkd->rkg", query_heads, fresh_keys, preferred_element_type=jnp.float32)
        * inv_root
    )
    visible = jnp.arange(slot_count, dtype=jnp.int32)[None, :] < lengths[:, None]
    visible = visible[:, None, None, :]
    cache_scores = jnp.where(visible, cache_scores, masked_score)
    row_max = jnp.maximum(jnp.max(cache_scores, axis=-1), fresh_scores)
    cache_exp = jnp.where(visible, jnp.exp(cache_scores - row_max[..., None]), 0.0)
    fresh_exp = jnp.exp(fresh_scores - row_max)
    denominator = jnp.sum(cache_exp, axis=-1) + fresh_exp
    cache_probs = (cache_exp / denominator[..., None]).astype(jnp.bfloat16)
    fresh_probs = (fresh_exp / denominator).astype(jnp.bfloat16)
    context = jnp.einsum(
        "rkgj,rjkd->rkgd", cache_probs, cache_values, preferred_element_type=jnp.float32
    )
    context = context + fresh_probs.astype(jnp.float32)[..., None] * fresh_values[:, :, None, :]
    return context.reshape(row_count, HEADS * HEAD_DIM)


def route_table(chosen_ids, logits):
    spread = logits[:, 0] - logits[:, 1]
    gates = jax.nn.sigmoid(jnp.stack([spread, -spread], axis=1))
    expert_range = jnp.arange(EXP_FLIGHT, dtype=jnp.int32)
    hits = (chosen_ids[:, :, None] == expert_range[None, None, :]).astype(jnp.float32)
    routed = jnp.sum(hits, axis=1)
    weight = jnp.sum(hits * gates[:, :, None], axis=1)
    return jnp.stack([routed, weight], axis=2)


def select_slots(routing, capacity):
    routed = routing[..., 0]
    position = jnp.cumsum(routed, axis=1) - routed
    places = jnp.arange(capacity, dtype=jnp.int32).astype(jnp.float32)
    selector = routed[..., None] * (position[..., None] == places).astype(jnp.float32)
    return jnp.transpose(selector, (0, 2, 3, 1))


def shards(
    hidden_in,
    queries,
    key_new,
    value_new,
    key_cache,
    value_cache,
    cache_length,
    expert_ids,
    route_logits,
    norm_gain,
    w_gate,
    w_up,
    w_down,
):
    micro_count = hidden_in.shape[0]
    own_rows = hidden_in.shape[1]
    model_width = hidden_in.shape[2]
    dev_count = lax.axis_size("dev")
    sub_count = lax.axis_size("sub")
    pair_rows = own_rows * sub_count
    capacity = pair_rows // 2 + 1
    half_width = model_width // sub_count
    per_expert = dev_count // EXP_FLIGHT
    block_hidden = w_gate.shape[1]
    block_index = lax.axis_index("dev")
    my_expert = block_index // per_expert
    results = []
    for micro_step in range(micro_count):
        context = attend(
            queries[micro_step],
            key_new[micro_step],
            value_new[micro_step],
            key_cache[micro_step],
            value_cache[micro_step],
            cache_length[micro_step],
        )
        resid = hidden_in[micro_step].astype(jnp.float32) + context
        inv_rms = lax.rsqrt(jnp.mean(resid * resid, axis=1, keepdims=True) + 1e-05)
        normed = (resid * inv_rms * norm_gain[None, :]).astype(jnp.bfloat16)
        routing = route_table(expert_ids[micro_step], route_logits[micro_step])
        every_row = lax.all_gather(normed, ("dev", "sub"), axis=0, tiled=True)
        every_route = lax.all_gather(routing, ("dev", "sub"), axis=0, tiled=True)
        column_part = lax.dynamic_slice_in_dim(
            every_row, lax.axis_index("sub") * half_width, half_width, 1
        )
        column_part = column_part.reshape(dev_count, pair_rows, half_width)
        every_block = every_route.reshape(dev_count, pair_rows, EXP_FLIGHT, 2)
        every_selector = select_slots(every_block, capacity)
        my_selector = lax.dynamic_index_in_dim(every_selector, my_expert, 1, keepdims=False)
        slot_rows = jnp.einsum(
            "bcp,bpw->bcw",
            my_selector.astype(jnp.bfloat16),
            column_part,
            preferred_element_type=jnp.float32,
        ).astype(jnp.bfloat16)
        pair_route = lax.dynamic_index_in_dim(every_block, block_index, 0, keepdims=False)
        pair_selector = lax.dynamic_index_in_dim(every_selector, block_index, 0, keepdims=False)
        slot_matrix = slot_rows.reshape(dev_count * capacity, half_width)
        gate_part = jnp.dot(slot_matrix, w_gate, preferred_element_type=jnp.float32)
        up_part = jnp.dot(slot_matrix, w_up, preferred_element_type=jnp.float32)
        gate_sum, up_sum = lax.psum((gate_part, up_part), "sub")
        hidden_units = (
            (jax.nn.silu(gate_sum) * up_sum)
            .astype(jnp.bfloat16)
            .reshape(dev_count, capacity, block_hidden)
        )
        expert_out = jnp.dot(
            hidden_units.reshape(dev_count * capacity, block_hidden),
            w_down,
            preferred_element_type=jnp.float32,
        )
        returned_parts = lax.all_to_all(
            expert_out.reshape(dev_count, capacity, half_width),
            "dev",
            split_axis=0,
            concat_axis=0,
            tiled=True,
        )
        returned = jnp.sum(
            returned_parts.reshape(EXP_FLIGHT, per_expert, capacity, half_width), axis=1
        )
        weights = pair_selector * jnp.transpose(pair_route[:, :, 1])[:, None, :]
        mixture_pair = jnp.einsum("ecp,ecw->pw", weights, returned, precision=lax.Precision.HIGHEST)
        mixture_own = lax.all_to_all(
            mixture_pair.reshape(sub_count, own_rows, half_width),
            "sub",
            split_axis=0,
            concat_axis=2,
            tiled=True,
        )
        results.append((resid + mixture_own.reshape(own_rows, model_width)).astype(jnp.bfloat16))
    return jnp.stack(results, axis=0)


def solution(mesh):
    return jax.shard_map(
        shards,
        mesh=mesh,
        in_specs=(
            P(None, ("groups", "dev", "sub"), None),
            P(None, ("groups", "dev", "sub"), None),
            P(None, ("groups", "dev", "sub"), None),
            P(None, ("groups", "dev", "sub"), None),
            P(None, ("groups", "dev", "sub"), None, None),
            P(None, ("groups", "dev", "sub"), None, None),
            P(None, ("groups", "dev", "sub")),
            P(None, ("groups", "dev", "sub"), None),
            P(None, ("groups", "dev", "sub"), None),
            P(),
            P("sub", "dev"),
            P("sub", "dev"),
            P("dev", "sub"),
        ),
        out_specs=P(None, ("groups", "dev", "sub"), None),
        check_vma=False,
    )
```

profile of v0, /device:TPU:0, one launch (start us, length us, event | category | flops | bytes accessed | tf_op | source)
XLA Modules:
  0.0 203.2 jit_solution(14984028208431893427)
XLA Ops:
  6.5 0.7 slice_bitcast_fusion.3
  7.2 0.7 slice_bitcast_fusion.2
  8.2 0.1 convert_reduce_fusion
  8.4 0.1 copy.68
  8.5 23.2 %all_gather.12 = f32[32,2,2]{2,1,0:T(2,128)S(1)} all-gather(f32[2,2,2]{2,1,0:T(2,128)S(1)} %copy.68), channel_id=1, replica_groups=mesh['groups'=2,'dev'=8,'sub'=2] {'dev','sub'}, dimensions={0}, use_global_device_ids=true | all-gather | bytes 544 | tf_op jit(solution)/shard_map/all_gather | solution.py:109
  31.6 0.1 copy.71
  31.7 0.2 copy.94
  32.0 0.1 copy.78
  32.1 17.5 %all_gather.14 = f32[32,2,2]{2,1,0:T(2,128)S(1)} all-gather(f32[2,2,2]{2,1,0:T(2,128)S(1)} %copy.78), channel_id=1, replica_groups=mesh['groups'=2,'dev'=8,'sub'=2] {'dev','sub'}, dimensions={0}, use_global_device_ids=true | all-gather | bytes 544 | tf_op jit(solution)/shard_map/all_gather | solution.py:109
  49.5 0.1 copy.81
  49.7 0.2 copy.96
  49.9 0.8 slice_bitcast_fusion.5
  50.6 0.7 fusion.55
  51.4 0.7 convert_bitcast_fusion.1
  52.1 0.3 reduce_window_sum.17
  52.5 0.3 reduce_window_sum.18
  53.0 0.1 copy.84
  53.1 0.1 copy.74
  53.2 0.8 fusion.54
  54.1 0.8 slice_convert_fusion.1
  55.0 1.1 fusion.52
  56.3 0.1 fusion.58
  56.4 0.3 fusion.56
  56.7 0.2 fusion.12
  56.9 0.1 fusion.61
  57.1 0.3 fusion.57
  57.4 0.2 fusion.13
  57.6 1.1 fusion.53
  58.8 0.3 multiply_reduce_fusion.1
  59.2 0.3 multiply_reduce_fusion
  59.6 0.9 fusion.28
  60.5 19.9 %all-gather = bf16[16,2,6144]{2,1,0:T(2,128)(2,1)S(1)} all-gather(bf16[1,2,6144]{2,1,0:T(2,128)(2,1)S(1)} %get-tuple-element.21), channel_id=1, replica_groups=mesh['groups'=2,'dev'=8,'sub'=2] {'dev','sub'}, dimensions={0}, use_global_device_ids=true | all-gather | bytes 417792 | tf_op jit(solution)/shard_map/all_gather | solution.py:108
  80.4 0.1 reshape.218
  80.7 0.2 convolution_convert_fusion.1
  80.9 0.1 reshape.199
  81.0 7.0 %fusion.60 = f32[24,2048]{1,0:T(8,128)} fusion(bf16[24,3072]{1,0:T(8,128)(2,1)S(1)} %reshape.199, bf16[3072,2048]{1,0:T(8,128)(2,1)} %param.24), kind=kOutput, calls=%fused_computation.130 | convolution fusion | flops 301989888 | bytes 12926976 | tf_op jit(solution)/shard_map/dot_general | solution.py:127
  88.0 7.0 %fusion.59 = f32[24,2048]{1,0:T(8,128)} fusion(bf16[24,3072]{1,0:T(8,128)(2,1)S(1)} %reshape.199, bf16[3072,2048]{1,0:T(8,128)(2,1)} %param.23), kind=kOutput, calls=%fused_computation.129 | convolution fusion | flops 301989888 | bytes 12926976 | tf_op jit(solution)/shard_map/dot_general | solution.py:126
  95.0 18.7 %all-gather.1 = bf16[16,2,6144]{2,1,0:T(2,128)(2,1)S(1)} all-gather(bf16[1,2,6144]{2,1,0:T(2,128)(2,1)S(1)} %get-tuple-element.22), channel_id=1, replica_groups=mesh['groups'=2,'dev'=8,'sub'=2] {'dev','sub'}, dimensions={0}, use_global_device_ids=true | all-gather | bytes 417792 | tf_op jit(solution)/shard_map/all_gather | solution.py:108
  113.7 0.1 reshape.220
  114.0 0.2 convolution_convert_fusion
  114.2 0.1 reshape.207
  114.4 7.0 %fusion.63 = f32[24,2048]{1,0:T(8,128)} fusion(bf16[24,3072]{1,0:T(8,128)(2,1)S(1)} %reshape.207, bf16[3072,2048]{1,0:T(8,128)(2,1)} %param.24), kind=kOutput, calls=%fused_computation.133 | convolution fusion | flops 301989888 | bytes 12926976 | tf_op jit(solution)/shard_map/dot_general | solution.py:127
  121.4 7.0 %fusion.62 = f32[24,2048]{1,0:T(8,128)} fusion(bf16[24,3072]{1,0:T(8,128)(2,1)S(1)} %reshape.207, bf16[3072,2048]{1,0:T(8,128)(2,1)} %param.23), kind=kOutput, calls=%fused_computation.132 | convolution fusion | flops 301989888 | bytes 12926976 | tf_op jit(solution)/shard_map/dot_general | solution.py:126
  128.4 0.1 copy.95
  128.6 0.1 copy.72
  128.8 17.4 %all-reduce.3.cloned.1.call-done = (f32[24,2048]{1,0:T(8,128)}, f32[24,2048]{1,0:T(8,128)}, f32[24,2048]{1,0:T(8,128)}, f32[24,2048]{1,0:T(8,128)}) async-done(((f32[24,2048]{1,0:T(8,128)}, f32[24,2048]{1,0:T(8,128)}, f32[24,2048]{1,0:T(8,128)}, f32[24,2048]{1,0:T(8,128)}), (f32[24,2048]{1,0:T(8,128)}, f32[24,2048]{1,0:T(8,128)}, f32[24,2048]{1,0:T(8,128)}, ...) | async-done | bytes 786448 | tf_op jit(solution)/shard_map/psum | solution.py:128
  146.2 6.6 %fusion.6 = f32[24,3072]{1,0:T(8,128)S(1)} fusion(bf16[2048,3072]{1,0:T(8,128)(2,1)} %param.25, f32[24,2048]{1,0:T(8,128)} %get-tuple-element.11, f32[24,2048]{1,0:T(8,128)} %get-tuple-element.12), kind=kOutput, calls=%fused_computation.18 | convolution fusion | flops 302284800 | bytes 13271040 | tf_op jit(solution)/shard_map/dot_general | solution.py:134
  152.8 0.9 reshape.200
  153.7 5.9 %all-to-all-start = ((f32[8,3,3072]{2,1,0:T(4,128)}), f32[8,3,3072]{2,1,0:T(4,128)S(1)}, u32[]{:S(2)}, u32[]{:S(2)}) async-start(f32[8,3,3072]{2,1,0:T(4,128)} %reshape.200), calls=%async_computation | async-start | bytes 786432 | tf_op jit(solution)/shard_map/all_to_all | solution.py:139
  159.6 6.3 %fusion.7 = f32[24,3072]{1,0:T(8,128)S(1)} fusion(bf16[2048,3072]{1,0:T(8,128)(2,1)} %param.25, f32[24,2048]{1,0:T(8,128)S(1)} %copy-done, f32[24,2048]{1,0:T(8,128)S(1)} %copy-done.1), kind=kOutput, calls=%fused_computation.19 | convolution fusion | flops 302284800 | bytes 13271040 | tf_op jit(solution)/shard_map/dot_general | solution.py:134
  165.9 0.9 reshape.208
  166.8 4.9 %all-to-all-done = f32[8,3,3072]{2,1,0:T(4,128)S(1)} async-done(((f32[8,3,3072]{2,1,0:T(4,128)}), f32[8,3,3072]{2,1,0:T(4,128)S(1)}, u32[]{:S(2)}, u32[]{:S(2)}) %all-to-all-start) | async-done | bytes 294944 | tf_op jit(solution)/shard_map/all_to_all | solution.py:139
  171.7 3.6 %all-to-all-start.2 = ((f32[8,3,3072]{2,1,0:T(4,128)}), f32[8,3,3072]{2,1,0:T(4,128)S(1)}, u32[]{:S(2)}, u32[]{:S(2)}) async-start(f32[8,3,3072]{2,1,0:T(4,128)} %reshape.208), calls=%async_computation.2 | async-start | bytes 786432 | tf_op jit(solution)/shard_map/all_to_all | solution.py:139
  175.4 0.1 copy.97
  175.6 0.1 copy.73
  175.7 0.1 copy.82
  175.8 0.1 copy.83
  175.9 1.0 convolution_bitcast_fusion.1
  176.9 10.3 %all-to-all-done.2 = f32[8,3,3072]{2,1,0:T(4,128)S(1)} async-done(((f32[8,3,3072]{2,1,0:T(4,128)}), f32[8,3,3072]{2,1,0:T(4,128)S(1)}, u32[]{:S(2)}, u32[]{:S(2)}) %all-to-all-start.2) | async-done | bytes 294944 | tf_op jit(solution)/shard_map/all_to_all | solution.py:139
  187.2 3.3 %all-to-all-start.1 = ((f32[2,2,3072]{2,1,0:T(2,128)}), f32[2,2,3072]{2,1,0:T(2,128)S(1)}, u32[]{:S(2)}, u32[]{:S(2)}) async-start(f32[2,2,3072]{2,1,0:T(2,128)} %convolution_bitcast_fusion.1), calls=%async_computation.1 | async-start | bytes 98304 | tf_op jit(solution)/shard_map/all_to_all | solution.py:151
  190.6 0.4 convolution_bitcast_fusion
  190.9 1.0 all-to-all-done.1
  191.9 3.8 %all_to_all.40 = f32[2,2,3072]{2,1,0:T(2,128)S(1)} all-to-all(f32[2,2,3072]{2,1,0:T(2,128)S(1)} %convolution_bitcast_fusion), channel_id=1, replica_groups=mesh['groups'=2,'dev'=8,'sub'=2] {'sub'}, dimensions={0} | all-to-all | bytes 98304 | tf_op jit(solution)/shard_map/all_to_all | solution.py:151
  195.7 0.6 copy-done.3
  (61 shorter events, 1.8 us)
Async XLA Ops:
  6.5 139.7 %all-reduce.3.cloned.1.call-start = ((), (), s32[]{:S(2)}) async-start(), calls=%async_computation.4 | async-start | bytes 1572864 | tf_op jit(solution)/shard_map/psum | solution.py:128
  146.2 13.4 %copy-start = (f32[24,2048]{1,0:T(8,128)S(1)}, f32[24,2048]{1,0:T(8,128)}, u32[]{:S(2)}) copy-start(f32[24,2048]{1,0:T(8,128)} %get-tuple-element.9) | copy-start | bytes 589828
  146.2 13.4 %copy-start.1 = (f32[24,2048]{1,0:T(8,128)S(1)}, f32[24,2048]{1,0:T(8,128)}, u32[]{:S(2)}) copy-start(f32[24,2048]{1,0:T(8,128)} %get-tuple-element.10) | copy-start | bytes 589828
  153.7 42.0 %copy-start.2 = (bf16[2,2,6144]{2,1,0:T(2,128)(2,1)S(1)}, bf16[2,2,6144]{2,1,0:T(2,128)(2,1)}, u32[]{:S(2)}) copy-start(bf16[2,2,6144]{2,1,0:T(2,128)(2,1)} %param.13) | copy-start | bytes 147460
  153.7 18.1 %all-to-all-start = ((f32[8,3,3072]{2,1,0:T(4,128)}), f32[8,3,3072]{2,1,0:T(4,128)S(1)}, u32[]{:S(2)}, u32[]{:S(2)}) async-start(f32[8,3,3072]{2,1,0:T(4,128)} %reshape.200), calls=%async_computation | async-start | bytes 786432 | tf_op jit(solution)/shard_map/all_to_all | solution.py:139
  171.7 15.5 %all-to-all-start.2 = ((f32[8,3,3072]{2,1,0:T(4,128)}), f32[8,3,3072]{2,1,0:T(4,128)S(1)}, u32[]{:S(2)}, u32[]{:S(2)}) async-start(f32[8,3,3072]{2,1,0:T(4,128)} %reshape.208), calls=%async_computation.2 | async-start | bytes 786432 | tf_op jit(solution)/shard_map/all_to_all | solution.py:139
  187.2 4.7 %all-to-all-start.1 = ((f32[2,2,3072]{2,1,0:T(2,128)}), f32[2,2,3072]{2,1,0:T(2,128)S(1)}, u32[]{:S(2)}, u32[]{:S(2)}) async-start(f32[2,2,3072]{2,1,0:T(2,128)} %convolution_bitcast_fusion.1), calls=%async_computation.1 | async-start | bytes 98304 | tf_op jit(solution)/shard_map/all_to_all | solution.py:151
  195.7 0.6 copy-start.3
Sparse Core Ops, SparseCore 0:
  128.5 17.6 all-reduce.2
where the time goes:
time: 204 us; the launch traced here: 203 us
  blocking collectives  83 us (41%)
  matrix products  44.3 us (22%)
  waiting for transfers between devices  33.6 us (16%)
  between operations  13.7 us (7%)
  starting transfers between devices  12.9 us (6%)
  local copies, waits for them, and re-layouts  11.5 us (6%)
  other arithmetic  4.26 us (2%)
    all_gather x2, blocking collectives, shards(): every_route = lax.all_gather(routing, ('dev', 'sub'), axis=0, tiled=True)  40.6 us
    all_gather x2, blocking collectives, shards(): every_row = lax.all_gather(normed, ('dev', 'sub'), axis=0, tiled=True)  38.6 us
    psum x1, waiting for transfers between devices, shards(): gate_sum, up_sum = lax.psum((gate_part, up_part), 'sub')  17.4 us
    all_to_all x2, waiting for transfers between devices, shards(): lax.all_to_all(expert_out.reshape(dev_count, capacity, half_width), 'dev'...  15.2 us
    dot_general x2, matrix products, shards(): gate_part = jnp.dot(slot_matrix, w_gate, preferred_element_type=jnp.float32)  14 us
    dot_general x2, matrix products, shards(): up_part = jnp.dot(slot_matrix, w_up, preferred_element_type=jnp.float32)  14 us
    dot_general x2, matrix products, shards(): jnp.dot(hidden_units.reshape(dev_count * capacity, block_hidden), w_down,...  12.9 us
    all_to_all x2, starting transfers between devices, shards(): lax.all_to_all(expert_out.reshape(dev_count, capacity, half_width), 'dev'...  9.58 us
  transfers between devices with their start and end apart: 4, of which 4 were waited for; matrix products, arithmetic and copies ran while one was open for 5% of the time, Pallas kernels for 0%

commit v1 on v0

v1 whole, which is shorter than its diff:
```python
import functools

import jax
import jax.numpy as jnp
from jax import lax
from jax.experimental import pallas as pl
from jax.experimental.pallas import tpu as pltpu
from jax.sharding import PartitionSpec as P

HEADS = 48
KV_HEADS = 8
HEAD_DIM = 128
GROUP = HEADS // KV_HEADS
EXP_FLIGHT = 2
PIECES = 4
RETURN_CHUNKS = 3

masked_score = -1e30
f32 = jnp.float32
bf16 = jnp.bfloat16


def permutation(senders, rows, inverse):
    size = senders * PIECES * rows
    i = lax.broadcasted_iota(jnp.int32, (size, size), 0)
    c = lax.broadcasted_iota(jnp.int32, (size, size), 1)
    if inverse:
        i, c = c, i
    row_bits = rows.bit_length() - 1
    sender_bits = senders.bit_length() - 1
    row = i & (rows - 1)
    sender = lax.shift_right_logical(i, row_bits) & (senders - 1)
    piece = lax.shift_right_logical(i, row_bits + sender_bits)
    at = sender * (PIECES * rows) + piece * rows + row
    return jnp.where(at == c, 1.0, 0.0).astype(f32).astype(bf16)


def layer_kernel(
    micro, own, dev_count, sub_count, chunk,
    hidden_ref, query_ref, knew_ref, vnew_ref, kcache_ref, vcache_ref, length_ref,
    ids_ref, logit_ref, gain_ref, wg_ref, wu_ref, wd_ref,
    out_ref,
    kbuf, vbuf, wg, wu, wd, qbig, ctx, resid, send, arrived, perm, perm_back,
    x, parts, other, units, acc, back, returned, result,
    kv_sem, wg_sem, wu_sem, wd_sem, send_sem, arrive_sem, part_sem, other_sem, back_sem, return_sem,
):
    rows = micro * own
    count = dev_count * sub_count
    my_dev = lax.axis_index("dev")
    my_sub = lax.axis_index("sub")
    me = my_dev * sub_count + my_sub
    half = wg.shape[1]
    piece = half // PIECES
    chunks = wg.shape[0]
    width = half // RETURN_CHUNKS
    small = width // PIECES
    group_width = GROUP * HEAD_DIM

    kv_copies = [
        pltpu.make_async_copy(kcache_ref, kbuf, kv_sem.at[0]),
        pltpu.make_async_copy(vcache_ref, vbuf, kv_sem.at[1]),
    ]
    for copy in kv_copies:
        copy.start()

    def wg_copy(n):
        cols = pl.ds(pl.multiple_of(n * chunk, chunk), chunk)
        return (
            pltpu.make_async_copy(wg_ref.at[:, cols], wg.at[n], wg_sem.at[n]),
            pltpu.make_async_copy(wu_ref.at[:, cols], wu.at[n], wu_sem.at[n]),
        )

    def wd_copy(n):
        return pltpu.make_async_copy(wd_ref.at[pl.ds(n * chunk, chunk)], wd.at[n], wd_sem.at[n])

    for n in range(chunks):
        for copy in wg_copy(n):
            copy.start()
    for n in range(chunks):
        wd_copy(n).start()

    def peer(offset):
        target = lax.rem(me + offset, count)
        return target, {"dev": target // sub_count, "sub": lax.rem(target, sub_count)}

    barrier = pltpu.get_barrier_semaphore()
    for offset in range(1, count):
        pl.semaphore_signal(
            barrier, inc=1, device_id=peer(offset)[1], device_id_type=pl.DeviceIdType.MESH
        )

    perm[...] = permutation(count, rows, False)
    perm_back[...] = permutation(count, rows, True)

    inv_root = 1.0 / HEAD_DIM**0.5
    qbig[...] = jnp.zeros_like(qbig)
    for r in range(rows):
        m, i = divmod(r, own)
        q = query_ref[m].astype(f32)
        for h in range(HEADS):
            k = h // GROUP
            qbig[r, h : h + 1, k * HEAD_DIM : (k + 1) * HEAD_DIM] = q[
                i : i + 1, h * HEAD_DIM : (h + 1) * HEAD_DIM
            ]
    for copy in kv_copies:
        copy.wait()
    slot = lax.broadcasted_iota(jnp.int32, (HEADS, kbuf.shape[2]), 1)
    for r in range(rows):
        m, i = divmod(r, own)
        q = qbig[r]
        scores = lax.dot_general(
            q.astype(bf16), kbuf[m, i], (((1,), (1,)), ((), ())), preferred_element_type=f32
        ) * inv_root
        new_key = knew_ref[m].astype(f32)[i : i + 1]
        new_value = vnew_ref[m].astype(f32)[i : i + 1]
        fresh = jnp.sum(q * new_key, axis=1, keepdims=True) * inv_root
        visible = slot < length_ref[m, i]
        scores = jnp.where(visible, scores, masked_score)
        top = jnp.maximum(jnp.max(scores, axis=1, keepdims=True), fresh)
        exps = jnp.where(visible, jnp.exp(scores - top), 0.0)
        fresh_exp = jnp.exp(fresh - top)
        total = jnp.sum(exps, axis=1, keepdims=True) + fresh_exp
        probs = (exps / total).astype(bf16)
        fresh_probs = (fresh_exp / total).astype(bf16).astype(f32)
        wide = jnp.dot(probs, vbuf[m, i], preferred_element_type=f32) + fresh_probs * new_value
        for h in range(HEADS):
            k, g = divmod(h, GROUP)
            ctx[k * rows + r : k * rows + r + 1, g * HEAD_DIM : (g + 1) * HEAD_DIM] = wide[
                h : h + 1, k * HEAD_DIM : (k + 1) * HEAD_DIM
            ]

    squares = jnp.zeros((rows, 1), f32)
    for k in range(KV_HEADS):
        cols = slice(k * group_width, (k + 1) * group_width)
        for m in range(micro):
            base = k * rows + m * own
            resid[m * own : (m + 1) * own, cols] = (
                hidden_ref[m, :, cols].astype(f32) + ctx[base : base + own, :]
            )
        value = resid[:, cols]
        squares = squares + jnp.sum(value * value, axis=1, keepdims=True)
    inv_rms = lax.rsqrt(squares / (KV_HEADS * group_width) + 1e-05)
    for k in range(KV_HEADS):
        cols = slice(k * group_width, (k + 1) * group_width)
        ctx[k * rows : (k + 1) * rows, :] = resid[:, cols] * inv_rms * gain_ref[:, cols]
    for s in range(sub_count):
        send[s] = ctx[s * PIECES * rows : (s + 1) * PIECES * rows, :].astype(bf16)

    pl.semaphore_wait(barrier, count - 1)

    def dispatch(offset):
        target, place = peer(offset)
        return pltpu.make_async_remote_copy(
            src_ref=send.at[lax.rem(target, sub_count)],
            dst_ref=arrived.at[me],
            send_sem=send_sem.at[offset],
            recv_sem=arrive_sem.at[offset],
            device_id=place,
            device_id_type=pl.DeviceIdType.MESH,
        )

    for offset in range(1, count):
        dispatch(offset).start()
    arrived[me] = send[my_sub]
    for offset in range(1, count):
        dispatch(offset).wait_recv()

    grid = arrived[...].reshape(count * PIECES * rows, piece)
    sorted_rows = jnp.dot(perm[...], grid, preferred_element_type=f32).astype(bf16)
    tall = count * rows
    for j in range(PIECES):
        x[:, j * piece : (j + 1) * piece] = sorted_rows[j * tall : (j + 1) * tall]

    def exchange(n):
        return pltpu.make_async_remote_copy(
            src_ref=parts.at[n],
            dst_ref=other.at[n],
            send_sem=part_sem.at[n],
            recv_sem=other_sem.at[n],
            device_id={"dev": my_dev, "sub": 1 - my_sub},
            device_id_type=pl.DeviceIdType.MESH,
        )

    def finish(n):
        exchange(n).wait_recv()
        gate = parts[n, 0] + other[n, 0]
        up = parts[n, 1] + other[n, 1]
        units[n] = (jax.nn.silu(gate) * up).astype(bf16)

    def gate_up(n, carry):
        for copy in wg_copy(n):
            copy.wait()
        parts[n, 0] = jnp.dot(x[...], wg[n], preferred_element_type=f32)
        parts[n, 1] = jnp.dot(x[...], wu[n], preferred_element_type=f32)
        exchange(n).start()

        @pl.when(n > 0)
        def _():
            finish(n - 1)

        return carry

    lax.fori_loop(0, chunks, gate_up, 0)

    for n in range(chunks):
        wd_copy(n).wait()

    def down(c, carry):
        cols = pl.ds(pl.multiple_of(c * width, width), width)
        total = jnp.zeros((tall, width), f32)
        for n in range(chunks - 1):
            total = total + jnp.dot(units[n], wd[n, :, cols], preferred_element_type=f32)
        acc[c] = total
        return carry

    if chunks > 1:
        lax.fori_loop(0, RETURN_CHUNKS, down, 0)
    finish(chunks - 1)

    def give_back(c, offset):
        target, place = peer(offset)
        return pltpu.make_async_remote_copy(
            src_ref=back.at[c, target],
            dst_ref=returned.at[c, me],
            send_sem=back_sem.at[c, offset],
            recv_sem=return_sem.at[c, offset],
            device_id=place,
            device_id_type=pl.DeviceIdType.MESH,
        )

    def last(c, carry):
        cols = pl.ds(pl.multiple_of(c * width, width), width)
        total = jnp.dot(units[chunks - 1], wd[chunks - 1, :, cols], preferred_element_type=f32)
        if chunks > 1:
            total = total + acc[c]
        total = total.astype(bf16)
        stacked = jnp.concatenate(
            [total[:, j * small : (j + 1) * small] for j in range(PIECES)], axis=0
        )
        sorted_out = jnp.dot(perm_back[...], stacked, preferred_element_type=f32).astype(bf16)
        back[c] = sorted_out.reshape(count, PIECES * rows, small)
        for offset in range(1, count):
            give_back(c, offset).start()
        returned[c, me] = back[c, me]
        return carry

    lax.fori_loop(0, RETURN_CHUNKS, last, 0)

    row_at = lax.broadcasted_iota(jnp.int32, (PIECES * rows, HEAD_DIM), 0) & (rows - 1)
    spread = jnp.zeros(row_at.shape, f32)
    first = jnp.full(row_at.shape, -1, jnp.int32)
    second = jnp.full(row_at.shape, -1, jnp.int32)
    for r in range(rows):
        m, i = divmod(r, own)
        spread = jnp.where(row_at == r, logit_ref[m, i, 0] - logit_ref[m, i, 1], spread)
        first = jnp.where(row_at == r, ids_ref[m, i, 0], first)
        second = jnp.where(row_at == r, ids_ref[m, i, 1], second)
    gate_first = jax.nn.sigmoid(spread)
    gate_second = jax.nn.sigmoid(-spread)
    weights = []
    for e in range(EXP_FLIGHT):
        weight = jnp.where(first == e, gate_first, 0.0) + jnp.where(second == e, gate_second, 0.0)
        weights.append(weight[:, :1])

    per_expert = dev_count // EXP_FLIGHT
    for c in range(RETURN_CHUNKS):
        for offset in range(1, count):
            give_back(c, offset).wait_recv()
        for s in range(sub_count):
            mixture = jnp.zeros((PIECES * rows, small), f32)
            for e in range(EXP_FLIGHT):
                expert_sum = jnp.zeros((PIECES * rows, small), f32)
                for b in range(e * per_expert, (e + 1) * per_expert):
                    expert_sum = expert_sum + returned[c, b * sub_count + s].astype(f32)
                mixture = mixture + weights[e] * expert_sum
            for j in range(PIECES):
                start = s * half + c * width + j * small
                cols = slice(start, start + small)
                result[:, cols] = resid[:, cols] + mixture[j * rows : (j + 1) * rows, :]
    for m in range(micro):
        out_ref[m] = result[m * own : (m + 1) * own, :].astype(bf16)

    for offset in range(1, count):
        dispatch(offset).wait_send()
    for n in range(chunks):
        exchange(n).wait_send()
    for c in range(RETURN_CHUNKS):
        for offset in range(1, count):
            give_back(c, offset).wait_send()


def shards(
    hidden_in, queries, key_new, value_new, key_cache, value_cache, cache_length,
    expert_ids, route_logits, norm_gain, w_gate, w_up, w_down,
):
    micro, own, model = hidden_in.shape
    slots = key_cache.shape[2]
    kv_width = key_cache.shape[3]
    dev_count = lax.axis_size("dev")
    sub_count = lax.axis_size("sub")
    count = dev_count * sub_count
    rows = micro * own
    tall = count * rows
    half, hidden = w_gate.shape
    chunk = min(512, hidden)
    chunks = hidden // chunk
    piece = half // PIECES
    width = half // RETURN_CHUNKS
    small = width // PIECES
    lane_rows = PIECES * rows
    vmem = pl.BlockSpec(memory_space=pltpu.VMEM)
    smem = pl.BlockSpec(memory_space=pltpu.SMEM)
    anywhere = pl.BlockSpec(memory_space=pl.ANY)
    dma = pltpu.SemaphoreType.DMA
    return pl.pallas_call(
        functools.partial(layer_kernel, micro, own, dev_count, sub_count, chunk),
        out_shape=jax.ShapeDtypeStruct((micro, own, model), bf16),
        in_specs=[
            vmem, vmem, vmem, vmem, anywhere, anywhere, smem, smem, smem, vmem,
            anywhere, anywhere, anywhere,
        ],
        out_specs=vmem,
        scratch_shapes=[
            pltpu.VMEM((micro, own, slots, kv_width), bf16),
            pltpu.VMEM((micro, own, slots, kv_width), bf16),
            pltpu.VMEM((chunks, half, chunk), bf16),
            pltpu.VMEM((chunks, half, chunk), bf16),
            pltpu.VMEM((chunks, chunk, half), bf16),
            pltpu.VMEM((rows, HEADS, kv_width), f32),
            pltpu.VMEM((KV_HEADS * rows, GROUP * HEAD_DIM), f32),
            pltpu.VMEM((rows, model), f32),
            pltpu.VMEM((sub_count, lane_rows, piece), bf16),
            pltpu.VMEM((count, lane_rows, piece), bf16),
            pltpu.VMEM((count * lane_rows, count * lane_rows), bf16),
            pltpu.VMEM((count * lane_rows, count * lane_rows), bf16),
            pltpu.VMEM((tall, half), bf16),
            pltpu.VMEM((chunks, 2, tall, chunk), f32),
            pltpu.VMEM((chunks, 2, tall, chunk), f32),
            pltpu.VMEM((chunks, tall, chunk), bf16),
            pltpu.VMEM((RETURN_CHUNKS, tall, width), f32),
            pltpu.VMEM((RETURN_CHUNKS, count, lane_rows, small), bf16),
            pltpu.VMEM((RETURN_CHUNKS, count, lane_rows, small), bf16),
            pltpu.VMEM((rows, model), f32),
            dma((2,)),
            dma((chunks,)),
            dma((chunks,)),
            dma((chunks,)),
            dma((count,)),
            dma((count,)),
            dma((chunks,)),
            dma((chunks,)),
            dma((RETURN_CHUNKS, count)),
            dma((RETURN_CHUNKS, count)),
        ],
        compiler_params=pltpu.CompilerParams(
            collective_id=0, has_side_effects=True, vmem_limit_bytes=56 * 2**20
        ),
    )(
        hidden_in, queries, key_new, value_new, key_cache, value_cache, cache_length,
        expert_ids, route_logits, norm_gain.reshape(1, model), w_gate, w_up, w_down,
    )


def solution(mesh):
    return jax.shard_map(
        shards,
        mesh=mesh,
        in_specs=(
            P(None, ("groups", "dev", "sub"), None),
            P(None, ("groups", "dev", "sub"), None),
            P(None, ("groups", "dev", "sub"), None),
            P(None, ("groups", "dev", "sub"), None),
            P(None, ("groups", "dev", "sub"), None, None),
            P(None, ("groups", "dev", "sub"), None, None),
            P(None, ("groups", "dev", "sub")),
            P(None, ("groups", "dev", "sub"), None),
            P(None, ("groups", "dev", "sub"), None),
            P(),
            P("sub", "dev"),
            P("sub", "dev"),
            P("dev", "sub"),
        ),
        out_specs=P(None, ("groups", "dev", "sub"), None),
        check_vma=False,
    )
```

time: 204 us -> 45.4 us (0.22)
  blocking collectives: 83 us -> 0 us
  matrix products: 44.3 us -> 0 us
  Pallas kernels: 0 us -> 43.7 us
  waiting for transfers between devices: 33.6 us -> 0 us
  between operations: 13.7 us -> 0.01 us
  starting transfers between devices: 12.9 us -> 0 us
  local copies, waits for them, and re-layouts: 11.5 us -> 1.45 us
  other arithmetic: 4.26 us -> 0 us
    all_gather x4 -> x0, blocking collectives: 79.2 us -> none  [the longest x2 40.6 us: shards(): every_route = lax.all_gather(routing, ('dev', 'sub'), axis=0, tiled=True)]
    dot_general x16 -> x0, matrix products: 44.3 us -> none  [the longest x2 14 us: shards(): gate_part = jnp.dot(slot_matrix, w_gate, preferred_element_type=jnp.float32)]
    pallas_call x0 -> x1, Pallas kernels: none -> 43.7 us  [shards(): pl.pallas_call(functools.partial(layer_kernel, micro, own, dev_count, sub...]
    psum x1 -> x0, waiting for transfers between devices: 17.4 us -> none  [shards(): gate_sum, up_sum = lax.psum((gate_part, up_part), 'sub')]
    all_to_all x3 -> x0, waiting for transfers between devices: 16.2 us -> none  [the longest x2 15.2 us: shards(): lax.all_to_all(expert_out.reshape(dev_count, capacity, half_width), 'dev'...]
    all_to_all x3 -> x0, starting transfers between devices: 12.9 us -> none  [the longest x2 9.58 us: shards(): lax.all_to_all(expert_out.reshape(dev_count, capacity, half_width), 'dev'...]
    slice x8 -> x0, local copies, waits for them, and re-layouts: 3.91 us -> none  [the longest x1 1.07 us: shards(): value_cache[micro_step]]
    all_to_all x1 -> x0, blocking collectives: 3.76 us -> none  [shards(): lax.all_to_all(mixture_pair.reshape(sub_count, own_rows, half_width), 'su...]
  transfers between devices with their start and end apart: 4 -> 0, of which waited for: 4 -> 0; matrix products, arithmetic and copies ran while one was open for 5% -> 0% of each run, Pallas kernels for 0% -> 0%
where the time goes in v1:
time: 45.4 us; the launch traced here: 45.1 us
  Pallas kernels  43.7 us (96%)
  local copies, waits for them, and re-layouts  1.45 us (3%)
    pallas_call x1, Pallas kernels, shards(): pl.pallas_call(functools.partial(layer_kernel, micro, own, dev_count, sub...  43.7 us
    unnamed x1, local copies, waits for them, and re-layouts  1.45 us

profile of v1, /device:TPU:0, one launch (start us, length us, event | category | flops | bytes accessed | tf_op | source)
XLA Modules:
  0.0 45.1 jit_solution(4919531586377910216)
XLA Ops:
  0.0 43.7 %shard_map.127 = bf16[2,2,6144]{2,1,0:T(2,128)(2,1)} custom-call(bf16[2,2,6144]{2,1,0:T(2,128)(2,1)} %hidden_ref.1, bf16[2,2,6144]{2,1,0:T(2,128)(2,1)} %query_ref.1, bf16[2,2,1024]{2,1,0:T(2,128)(2,1)} %knew_ref.1, bf16[2,2,1024]{2,1,0:T(2,128)(2,1)} %vnew_ref.1, bf16[2,2,64,1024]{3,2,1,0:T(8,128)(2,1)} %kcache_ref.1, bf16[2,2,64,1024]{3,2,1,0:T(8,128)(2,1)} %vcache_ref.1, ...), custom_call_target="tpu_custom_call" | custom-call | tf_op jit(solution)/shard_map/pallas_call | solution.py:315
  43.7 1.5 %copy.15 = bf16[2,2,6144]{2,1,0:T(2,128)(2,1)} copy(bf16[2,2,6144]{2,1,0:T(2,128)(2,1)} %shard_map.127) | data formatting | bytes 98304

commit v2 on v1

--- a/solution.py
+++ b/solution.py
@@ -75,9 +75,9 @@
 
     for n in range(chunks):
         for copy in wg_copy(n):
-            copy.start()
+            copy.start(priority=1)
     for n in range(chunks):
-        wd_copy(n).start()
+        wd_copy(n).start(priority=1)
 
     def peer(offset):
         target = lax.rem(me + offset, count)

time: 45.4 us -> 37.6 us (0.83)
  Pallas kernels: 43.7 us -> 35.9 us
    pallas_call x1, Pallas kernels: 43.7 us -> 35.9 us  [shards(): pl.pallas_call(functools.partial(layer_kernel, micro, own, dev_count, sub...]
where the time goes in v2:
time: 37.6 us; the launch traced here: 37.3 us
  Pallas kernels  35.9 us (95%)
  local copies, waits for them, and re-layouts  1.45 us (4%)
    pallas_call x1, Pallas kernels, shards(): pl.pallas_call(functools.partial(layer_kernel, micro, own, dev_count, sub...  35.9 us
    unnamed x1, local copies, waits for them, and re-layouts  1.45 us

profile of v2, /device:TPU:0, one launch (start us, length us, event | category | flops | bytes accessed | tf_op | source)
XLA Modules:
  0.0 37.3 jit_solution(3345638017530349100)
XLA Ops:
  0.0 35.9 %shard_map.127 = bf16[2,2,6144]{2,1,0:T(2,128)(2,1)} custom-call(bf16[2,2,6144]{2,1,0:T(2,128)(2,1)} %hidden_ref.1, bf16[2,2,6144]{2,1,0:T(2,128)(2,1)} %query_ref.1, bf16[2,2,1024]{2,1,0:T(2,128)(2,1)} %knew_ref.1, bf16[2,2,1024]{2,1,0:T(2,128)(2,1)} %vnew_ref.1, bf16[2,2,64,1024]{3,2,1,0:T(8,128)(2,1)} %kcache_ref.1, bf16[2,2,64,1024]{3,2,1,0:T(8,128)(2,1)} %vcache_ref.1, ...), custom_call_target="tpu_custom_call" | custom-call | tf_op jit(solution)/shard_map/pallas_call | solution.py:315
  35.9 1.5 %copy.15 = bf16[2,2,6144]{2,1,0:T(2,128)(2,1)} copy(bf16[2,2,6144]{2,1,0:T(2,128)(2,1)} %shard_map.127) | data formatting | bytes 98304

commit v3 on v2

v3 whole, which is shorter than its diff:
```python
import functools

import jax
import jax.numpy as jnp
from jax import lax
from jax.experimental import pallas as pl
from jax.experimental.pallas import tpu as pltpu
from jax.sharding import PartitionSpec as P

HEADS = 48
KV_HEADS = 8
HEAD_DIM = 128
GROUP = HEADS // KV_HEADS
EXP_FLIGHT = 2
PIECES = 4
CHUNKS = 3

masked_score = -1e30
f32 = jnp.float32
bf16 = jnp.bfloat16


def permutation(devs, subs, rows, per, inverse):
    senders = devs * subs
    size = senders * PIECES * rows
    i = lax.broadcasted_iota(jnp.int32, (size, size), 0)
    c = lax.broadcasted_iota(jnp.int32, (size, size), 1)
    if inverse:
        i, c = c, i
    row_bits = rows.bit_length() - 1
    sender_bits = senders.bit_length() - 1
    sub_bits = subs.bit_length() - 1
    row = i & (rows - 1)
    sender = lax.shift_right_logical(i, row_bits) & (senders - 1)
    piece = lax.shift_right_logical(i, row_bits + sender_bits)
    if inverse:
        dev = lax.shift_right_logical(sender, sub_bits)
        group = lax.shift_right_logical(dev, per.bit_length() - 1)
        sender = ((dev & (per - 1)) * EXP_FLIGHT + group) * subs + (sender & (subs - 1))
    at = sender * (PIECES * rows) + piece * rows + row
    return jnp.where(at == c, 1.0, 0.0).astype(f32).astype(bf16)


def layer_kernel(
    micro, own, dev_count, sub_count, chunk,
    hidden_ref, query_ref, knew_ref, vnew_ref, kcache_ref, vcache_ref, length_ref,
    ids_ref, logit_ref, gain_ref, wg_ref, wu_ref, wd_ref,
    out_ref,
    kbuf, vbuf, wg, wu, wd, qbig, ctx, resid, stage, send, arrived, perm, perm_back,
    x, parts, other, units, acc, back, partial, summed, returned, result,
    kv_sem, wg_sem, wu_sem, wd_sem, far_send, far_recv, pair_send, pair_recv, near_send, near_recv,
    fwd_send, fwd_recv, part_sem, other_sem, scatter_send, scatter_recv,
    home_send, home_recv, away_send, away_recv,
):
    rows = micro * own
    count = dev_count * sub_count
    my_dev = lax.axis_index("dev")
    my_sub = lax.axis_index("sub")
    me = my_dev * sub_count + my_sub
    per = dev_count // EXP_FLIGHT
    my_group = my_dev // per
    my_place = lax.rem(my_dev, per)
    far = lax.rem(my_dev + per, dev_count)
    half = wg.shape[0]
    chunks = wd.shape[0]
    width = half // CHUNKS
    small = width // PIECES
    group_width = GROUP * HEAD_DIM

    kv_copies = [
        pltpu.make_async_copy(kcache_ref, kbuf, kv_sem.at[0]),
        pltpu.make_async_copy(vcache_ref, vbuf, kv_sem.at[1]),
    ]
    for copy in kv_copies:
        copy.start()

    def wg_copy(c):
        at = pl.ds(c * width, width)
        return (
            pltpu.make_async_copy(wg_ref.at[at], wg.at[at], wg_sem.at[c]),
            pltpu.make_async_copy(wu_ref.at[at], wu.at[at], wu_sem.at[c]),
        )

    def wd_copy(n):
        return pltpu.make_async_copy(wd_ref.at[pl.ds(n * chunk, chunk)], wd.at[n], wd_sem.at[n])

    for c in range(CHUNKS):
        for copy in wg_copy(c):
            copy.start(priority=1)
    for n in range(chunks):
        wd_copy(n).start(priority=1)

    def near(offset):
        return my_group * per + lax.rem(my_place + offset, per)

    def push(src, dst, send_sem, recv_sem, dev, sub):
        return pltpu.make_async_remote_copy(
            src_ref=src,
            dst_ref=dst,
            send_sem=send_sem,
            recv_sem=recv_sem,
            device_id={"dev": dev, "sub": sub},
            device_id_type=pl.DeviceIdType.MESH,
        )

    other_sub = 1 - my_sub
    barrier = pltpu.get_barrier_semaphore()
    peers = [(far, t) for t in range(sub_count)] + [(my_dev, other_sub)]
    peers += [(near(o), t) for o in range(1, per) for t in range(sub_count)]
    for dev, sub in peers:
        pl.semaphore_signal(
            barrier, inc=1, device_id={"dev": dev, "sub": sub},
            device_id_type=pl.DeviceIdType.MESH,
        )

    perm[...] = permutation(dev_count, sub_count, rows, per, False)
    perm_back[...] = permutation(dev_count, sub_count, rows, per, True)

    inv_root = 1.0 / HEAD_DIM**0.5
    qbig[...] = jnp.zeros_like(qbig)
    for r in range(rows):
        m, i = divmod(r, own)
        q = query_ref[m].astype(f32)
        for h in range(HEADS):
            k = h // GROUP
            qbig[r, h : h + 1, k * HEAD_DIM : (k + 1) * HEAD_DIM] = q[
                i : i + 1, h * HEAD_DIM : (h + 1) * HEAD_DIM
            ]
    for copy in kv_copies:
        copy.wait()
    slot = lax.broadcasted_iota(jnp.int32, (HEADS, kbuf.shape[2]), 1)
    for r in range(rows):
        m, i = divmod(r, own)
        q = qbig[r]
        scores = lax.dot_general(
            q.astype(bf16), kbuf[m, i], (((1,), (1,)), ((), ())), preferred_element_type=f32
        ) * inv_root
        new_key = knew_ref[m].astype(f32)[i : i + 1]
        new_value = vnew_ref[m].astype(f32)[i : i + 1]
        fresh = jnp.sum(q * new_key, axis=1, keepdims=True) * inv_root
        visible = slot < length_ref[m, i]
        scores = jnp.where(visible, scores, masked_score)
        top = jnp.maximum(jnp.max(scores, axis=1, keepdims=True), fresh)
        exps = jnp.where(visible, jnp.exp(scores - top), 0.0)
        fresh_exp = jnp.exp(fresh - top)
        total = jnp.sum(exps, axis=1, keepdims=True) + fresh_exp
        probs = (exps / total).astype(bf16)
        fresh_probs = (fresh_exp / total).astype(bf16).astype(f32)
        wide = jnp.dot(probs, vbuf[m, i], preferred_element_type=f32) + fresh_probs * new_value
        for h in range(HEADS):
            k, g = divmod(h, GROUP)
            ctx[k * rows + r : k * rows + r + 1, g * HEAD_DIM : (g + 1) * HEAD_DIM] = wide[
                h : h + 1, k * HEAD_DIM : (k + 1) * HEAD_DIM
            ]

    squares = jnp.zeros((rows, 1), f32)
    for k in range(KV_HEADS):
        cols = slice(k * group_width, (k + 1) * group_width)
        for m in range(micro):
            base = k * rows + m * own
            resid[m * own : (m + 1) * own, cols] = (
                hidden_ref[m, :, cols].astype(f32) + ctx[base : base + own, :]
            )
        value = resid[:, cols]
        squares = squares + jnp.sum(value * value, axis=1, keepdims=True)
    inv_rms = lax.rsqrt(squares / (KV_HEADS * group_width) + 1e-05)
    for s in range(sub_count):
        for c in range(CHUNKS):
            for j in range(PIECES):
                start = s * half + c * width + j * small
                cols = slice(start, start + small)
                stage[s, c, j * rows : (j + 1) * rows, :] = (
                    resid[:, cols] * inv_rms * gain_ref[:, cols]
                )
    send[...] = stage[...].astype(bf16)

    pl.semaphore_wait(barrier, len(peers))

    def to_far(c, t):
        return push(
            send.at[t, c], arrived.at[c, me], far_send.at[c, t], far_recv.at[c, my_sub], far, t
        )

    def from_far(c, t):
        return push(
            send.at[t, c], arrived.at[c, me], far_send.at[c, t], far_recv.at[c, t], far, t
        )

    def to_pair(c):
        return push(
            send.at[other_sub, c], arrived.at[c, me], pair_send.at[c], pair_recv.at[c],
            my_dev, other_sub,
        )

    def to_near(c, o, t):
        return push(
            send.at[t, c], arrived.at[c, me], near_send.at[c, o, t], near_recv.at[c, o, my_sub],
            near(o), t,
        )

    def from_near(c, o, t):
        return push(
            send.at[t, c], arrived.at[c, me], near_send.at[c, o, t], near_recv.at[c, o, t],
            near(o), t,
        )

    def hand_on(c, o):
        at = pl.ds(far * sub_count, sub_count)
        return push(
            arrived.at[c, at], arrived.at[c, at], fwd_send.at[c, o], fwd_recv.at[c, o],
            near(o), my_sub,
        )

    for c in range(CHUNKS):
        for t in range(sub_count):
            to_far(c, t).start()
        for o in range(1, per):
            for t in range(sub_count):
                to_near(c, o, t).start()
        to_pair(c).start()
        arrived[c, me] = send[my_sub, c]
    for c in range(CHUNKS):
        for t in range(sub_count):
            from_far(c, t).wait_recv()
        for o in range(1, per):
            hand_on(c, o).start()

    tall = count * rows

    def exchange(n):
        return push(
            parts.at[n], other.at[n], part_sem.at[n], other_sem.at[n], my_dev, other_sub
        )

    def finish(n):
        exchange(n).wait_recv()
        gate = parts[n, 0] + other[n, 0]
        up = parts[n, 1] + other[n, 1]
        units[n] = (jax.nn.silu(gate) * up).astype(bf16)

    for c in range(CHUNKS):
        to_pair(c).wait_recv()
        for o in range(1, per):
            for t in range(sub_count):
                from_near(c, o, t).wait_recv()
            hand_on(c, o).wait_recv()
        grid = arrived[c].reshape(count * PIECES * rows, small)
        sorted_rows = jnp.dot(perm[...], grid, preferred_element_type=f32).astype(bf16)
        for j in range(PIECES):
            x[:, j * small : (j + 1) * small] = sorted_rows[j * tall : (j + 1) * tall]
        for copy in wg_copy(c):
            copy.wait()

        def gate_up(n, carry):
            at = slice(c * width, (c + 1) * width)
            cols = pl.ds(pl.multiple_of(n * chunk, chunk), chunk)
            gate = jnp.dot(x[...], wg[at, cols], preferred_element_type=f32)
            up = jnp.dot(x[...], wu[at, cols], preferred_element_type=f32)
            if c > 0:
                gate = gate + parts[n, 0]
                up = up + parts[n, 1]
            parts[n, 0] = gate
            parts[n, 1] = up
            if c == CHUNKS - 1:
                exchange(n).start()

                @pl.when(n > 0)
                def _():
                    finish(n - 1)

            return carry

        lax.fori_loop(0, chunks, gate_up, 0)

    for n in range(chunks):
        wd_copy(n).wait()

    def down(c, carry):
        cols = pl.ds(pl.multiple_of(c * width, width), width)
        total = jnp.zeros((tall, width), f32)
        for n in range(chunks - 1):
            total = total + jnp.dot(units[n], wd[n, :, cols], preferred_element_type=f32)
        acc[c] = total
        return carry

    if chunks > 1:
        lax.fori_loop(0, CHUNKS, down, 0)
    finish(chunks - 1)

    blocks = EXP_FLIGHT * sub_count

    def scatter(c, o):
        return push(
            back.at[c, pl.ds(lax.rem(my_place + o, per) * blocks, blocks)],
            partial.at[c, o], scatter_send.at[c, o], scatter_recv.at[c, o], near(o), my_sub,
        )

    landing = my_group * sub_count + my_sub

    def go_home(c):
        return push(
            summed.at[c, my_group * sub_count + other_sub], returned.at[c, landing],
            home_send.at[c], home_recv.at[c], my_dev, other_sub,
        )

    def go_away(c, t):
        return push(
            summed.at[c, (1 - my_group) * sub_count + t], returned.at[c, landing],
            away_send.at[c, t], away_recv.at[c, my_sub], far, t,
        )

    def come_away(c, t):
        return push(
            summed.at[c, (1 - my_group) * sub_count + t], returned.at[c, landing],
            away_send.at[c, t], away_recv.at[c, t], far, t,
        )

    def send_sums(c):
        for o in range(1, per):
            scatter(c, o).wait_recv()
        total = back[c, pl.ds(my_place * blocks, blocks)].astype(f32)
        for o in range(1, per):
            total = total + partial[c, o].astype(f32)
        summed[c] = total.astype(bf16)
        for t in range(sub_count):
            go_away(c, t).start()
        go_home(c).start()
        returned[c, landing] = summed[c, landing]

    for c in range(CHUNKS):
        cols = slice(c * width, (c + 1) * width)
        total = jnp.dot(units[chunks - 1], wd[chunks - 1, :, cols], preferred_element_type=f32)
        if chunks > 1:
            total = total + acc[c]
        total = total.astype(bf16)
        stacked = jnp.concatenate(
            [total[:, j * small : (j + 1) * small] for j in range(PIECES)], axis=0
        )
        sorted_out = jnp.dot(perm_back[...], stacked, preferred_element_type=f32).astype(bf16)
        back[c] = sorted_out.reshape(count, PIECES * rows, small)
        for o in range(1, per):
            scatter(c, o).start()
        if c > 0:
            send_sums(c - 1)
    send_sums(CHUNKS - 1)

    row_at = lax.broadcasted_iota(jnp.int32, (PIECES * rows, HEAD_DIM), 0) & (rows - 1)
    spread = jnp.zeros(row_at.shape, f32)
    first = jnp.full(row_at.shape, -1, jnp.int32)
    second = jnp.full(row_at.shape, -1, jnp.int32)
    for r in range(rows):
        m, i = divmod(r, own)
        spread = jnp.where(row_at == r, logit_ref[m, i, 0] - logit_ref[m, i, 1], spread)
        first = jnp.where(row_at == r, ids_ref[m, i, 0], first)
        second = jnp.where(row_at == r, ids_ref[m, i, 1], second)
    gate_first = jax.nn.sigmoid(spread)
    gate_second = jax.nn.sigmoid(-spread)
    weights = []
    for e in range(EXP_FLIGHT):
        weight = jnp.where(first == e, gate_first, 0.0) + jnp.where(second == e, gate_second, 0.0)
        weights.append(weight[:, :1])

    for c in range(CHUNKS):
        go_home(c).wait_recv()
        for t in range(sub_count):
            come_away(c, t).wait_recv()
        for s in range(sub_count):
            mixture = jnp.zeros((PIECES * rows, small), f32)
            for e in range(EXP_FLIGHT):
                mixture = mixture + weights[e] * returned[c, e * sub_count + s].astype(f32)
            for j in range(PIECES):
                start = s * half + c * width + j * small
                cols = slice(start, start + small)
                result[:, cols] = resid[:, cols] + mixture[j * rows : (j + 1) * rows, :]
    for m in range(micro):
        out_ref[m] = result[m * own : (m + 1) * own, :].astype(bf16)

    for n in range(chunks):
        exchange(n).wait_send()
    for c in range(CHUNKS):
        to_pair(c).wait_send()
        go_home(c).wait_send()
        for t in range(sub_count):
            to_far(c, t).wait_send()
            go_away(c, t).wait_send()
        for o in range(1, per):
            hand_on(c, o).wait_send()
            scatter(c, o).wait_send()
            for t in range(sub_count):
                to_near(c, o, t).wait_send()


def shards(
    hidden_in, queries, key_new, value_new, key_cache, value_cache, cache_length,
    expert_ids, route_logits, norm_gain, w_gate, w_up, w_down,
):
    micro, own, model = hidden_in.shape
    slots = key_cache.shape[2]
    kv_width = key_cache.shape[3]
    dev_count = lax.axis_size("dev")
    sub_count = lax.axis_size("sub")
    count = dev_count * sub_count
    rows = micro * own
    tall = count * rows
    half, hidden = w_gate.shape
    chunk = min(512, hidden)
    chunks = hidden // chunk
    per = dev_count // EXP_FLIGHT
    blocks = EXP_FLIGHT * sub_count
    width = half // CHUNKS
    small = width // PIECES
    lane_rows = PIECES * rows
    vmem = pl.BlockSpec(memory_space=pltpu.VMEM)
    smem = pl.BlockSpec(memory_space=pltpu.SMEM)
    anywhere = pl.BlockSpec(memory_space=pl.ANY)
    dma = pltpu.SemaphoreType.DMA
    return pl.pallas_call(
        functools.partial(layer_kernel, micro, own, dev_count, sub_count, chunk),
        out_shape=jax.ShapeDtypeStruct((micro, own, model), bf16),
        in_specs=[
            vmem, vmem, vmem, vmem, anywhere, anywhere, smem, smem, smem, vmem,
            anywhere, anywhere, anywhere,
        ],
        out_specs=vmem,
        scratch_shapes=[
            pltpu.VMEM((micro, own, slots, kv_width), bf16),
            pltpu.VMEM((micro, own, slots, kv_width), bf16),
            pltpu.VMEM((half, hidden), bf16),
            pltpu.VMEM((half, hidden), bf16),
            pltpu.VMEM((chunks, chunk, half), bf16),
            pltpu.VMEM((rows, HEADS, kv_width), f32),
            pltpu.VMEM((KV_HEADS * rows, GROUP * HEAD_DIM), f32),
            pltpu.VMEM((rows, model), f32),
            pltpu.VMEM((sub_count, CHUNKS, lane_rows, small), f32),
            pltpu.VMEM((sub_count, CHUNKS, lane_rows, small), bf16),
            pltpu.VMEM((CHUNKS, count, lane_rows, small), bf16),
            pltpu.VMEM((count * lane_rows, count * lane_rows), bf16),
            pltpu.VMEM((count * lane_rows, count * lane_rows), bf16),
            pltpu.VMEM((tall, width), bf16),
            pltpu.VMEM((chunks, 2, tall, chunk), f32),
            pltpu.VMEM((chunks, 2, tall, chunk), f32),
            pltpu.VMEM((chunks, tall, chunk), bf16),
            pltpu.VMEM((CHUNKS, tall, width), f32),
            pltpu.VMEM((CHUNKS, count, lane_rows, small), bf16),
            pltpu.VMEM((CHUNKS, per, blocks, lane_rows, small), bf16),
            pltpu.VMEM((CHUNKS, blocks, lane_rows, small), bf16),
            pltpu.VMEM((CHUNKS, blocks, lane_rows, small), bf16),
            pltpu.VMEM((rows, model), f32),
            dma((2,)),
            dma((CHUNKS,)),
            dma((CHUNKS,)),
            dma((chunks,)),
            dma((CHUNKS, sub_count)),
            dma((CHUNKS, sub_count)),
            dma((CHUNKS,)),
            dma((CHUNKS,)),
            dma((CHUNKS, per, sub_count)),
            dma((CHUNKS, per, sub_count)),
            dma((CHUNKS, per)),
            dma((CHUNKS, per)),
            dma((chunks,)),
            dma((chunks,)),
            dma((CHUNKS, per)),
            dma((CHUNKS, per)),
            dma((CHUNKS,)),
            dma((CHUNKS,)),
            dma((CHUNKS, sub_count)),
            dma((CHUNKS, sub_count)),
        ],
        compiler_params=pltpu.CompilerParams(
            collective_id=0, has_side_effects=True, vmem_limit_bytes=56 * 2**20
        ),
    )(
        hidden_in, queries, key_new, value_new, key_cache, value_cache, cache_length,
        expert_ids, route_logits, norm_gain.reshape(1, model), w_gate, w_up, w_down,
    )


def solution(mesh):
    return jax.shard_map(
        shards,
        mesh=mesh,
        in_specs=(
            P(None, ("groups", "dev", "sub"), None),
            P(None, ("groups", "dev", "sub"), None),
            P(None, ("groups", "dev", "sub"), None),
            P(None, ("groups", "dev", "sub"), None),
            P(None, ("groups", "dev", "sub"), None, None),
            P(None, ("groups", "dev", "sub"), None, None),
            P(None, ("groups", "dev", "sub")),
            P(None, ("groups", "dev", "sub"), None),
            P(None, ("groups", "dev", "sub"), None),
            P(),
            P("sub", "dev"),
            P("sub", "dev"),
            P("dev", "sub"),
        ),
        out_specs=P(None, ("groups", "dev", "sub"), None),
        check_vma=False,
    )
```

time: 37.6 us -> 39.1 us (1.040)
  Pallas kernels: 35.9 us -> 37.5 us
    pallas_call x1, Pallas kernels: 35.9 us -> 37.5 us  [shards(): pl.pallas_call(functools.partial(layer_kernel, micro, own, dev_count, sub...]
where the time goes in v3:
time: 39.1 us; the launch traced here: 38.9 us
  Pallas kernels  37.5 us (96%)
  local copies, waits for them, and re-layouts  1.45 us (4%)
    pallas_call x1, Pallas kernels, shards(): pl.pallas_call(functools.partial(layer_kernel, micro, own, dev_count, sub...  37.5 us
    unnamed x1, local copies, waits for them, and re-layouts  1.45 us

profile of v3, /device:TPU:0, one launch (start us, length us, event | category | flops | bytes accessed | tf_op | source)
XLA Modules:
  0.0 38.9 jit_solution(14058410160928093939)
XLA Ops:
  0.0 37.5 %shard_map.127 = bf16[2,2,6144]{2,1,0:T(2,128)(2,1)} custom-call(bf16[2,2,6144]{2,1,0:T(2,128)(2,1)} %hidden_ref.1, bf16[2,2,6144]{2,1,0:T(2,128)(2,1)} %query_ref.1, bf16[2,2,1024]{2,1,0:T(2,128)(2,1)} %knew_ref.1, bf16[2,2,1024]{2,1,0:T(2,128)(2,1)} %vnew_ref.1, bf16[2,2,64,1024]{3,2,1,0:T(8,128)(2,1)} %kcache_ref.1, bf16[2,2,64,1024]{3,2,1,0:T(8,128)(2,1)} %vcache_ref.1, ...), custom_call_target="tpu_custom_call" | custom-call | tf_op jit(solution)/shard_map/pallas_call | solution.py:417
  37.5 1.5 %copy.15 = bf16[2,2,6144]{2,1,0:T(2,128)(2,1)} copy(bf16[2,2,6144]{2,1,0:T(2,128)(2,1)} %shard_map.127) | data formatting | bytes 98304

commit v4 on v2

--- a/solution.py
+++ b/solution.py
@@ -13,7 +13,7 @@
 GROUP = HEADS // KV_HEADS
 EXP_FLIGHT = 2
 PIECES = 4
-RETURN_CHUNKS = 3
+RETURN_CHUNKS = 1
 
 masked_score = -1e30
 f32 = jnp.float32

time: 37.6 us -> 35.4 us (0.941)
  the two profiles are of different devices: /device:TPU:0 before, /device:TPU:29 now
where the time goes in v4:
time: 35.4 us; the launch traced here: 35.2 us
  Pallas kernels  33.7 us (95%)
  local copies, waits for them, and re-layouts  1.45 us (4%)
    pallas_call x1, Pallas kernels, shards(): pl.pallas_call(functools.partial(layer_kernel, micro, own, dev_count, sub...  33.7 us
    unnamed x1, local copies, waits for them, and re-layouts  1.45 us

profile of v4, /device:TPU:29, one launch (start us, length us, event | category | flops | bytes accessed | tf_op | source)
XLA Modules:
  0.0 35.2 jit_solution(9349795556132761995)
XLA Ops:
  0.0 33.7 %shard_map.127 = bf16[2,2,6144]{2,1,0:T(2,128)(2,1)} custom-call(bf16[2,2,6144]{2,1,0:T(2,128)(2,1)} %hidden_ref.1, bf16[2,2,6144]{2,1,0:T(2,128)(2,1)} %query_ref.1, bf16[2,2,1024]{2,1,0:T(2,128)(2,1)} %knew_ref.1, bf16[2,2,1024]{2,1,0:T(2,128)(2,1)} %vnew_ref.1, bf16[2,2,64,1024]{3,2,1,0:T(8,128)(2,1)} %kcache_ref.1, bf16[2,2,64,1024]{3,2,1,0:T(8,128)(2,1)} %vcache_ref.1, ...), custom_call_target="tpu_custom_call" | custom-call | tf_op jit(solution)/shard_map/pallas_call | solution.py:315
  33.7 1.5 %copy.15 = bf16[2,2,6144]{2,1,0:T(2,128)(2,1)} copy(bf16[2,2,6144]{2,1,0:T(2,128)(2,1)} %shard_map.127) | data formatting | bytes 98304
